TPU v7x, 32 devices: a whole 2x2x4 slice. The times are simulated.
32 devices in a mesh: grp: 1, dom: 32 (over z, y, x, core).
Axes of the slice: x: 2, y: 2, z: 4, core: 2. Of those that a mesh axis runs over, the one named last changes fastest.
Arguments:
- owned_blips: bfloat16 [128, 32768], P(('grp', 'dom')), may hold values from -6 to 6
- potential: float32 [32, 32, 1024], P('dom', 'grp'), may hold values from -5 to 5
- slot_owner: int32 [768, 1], P(('grp', 'dom')), may hold values from 0 to 31; in each aligned block of 24 rows (0 to 23, 24 to 47, ...) at most 2 rows name the same one
- slot_row: int32 [768], P(('grp', 'dom')), may hold values from 0 to 3
- slot_offset: int32 [768], P(('grp', 'dom')), may hold values from 0 to 31
Outputs:
- blip_gradient: float32 [128, 32768], P(('grp', 'dom'))
- hamiltonian: float32 [128, 128], P(('grp', 'dom'))
Inputs may be any that keep to these rules, and one draw needn't show every extreme that they name: `slot_owner`: among the 24 pieces of one device at most 2 name the same owner.
All inputs are finite; a program needn't handle non-finite values.
Results may differ from a plain program's by a relative error of at most 0.012.
The roundings to bfloat16 on the way count: a program that leaves them out, or rounds other values in their place, can miss the bound.
Values may be sent and summed in bfloat16 or wider, within the bound.
A program may use at most 128 MiB of HBM per device.

v0:
```python
import jax
import jax.numpy as jnp
from jax import lax
from jax.sharding import PartitionSpec as P

NB = 32


def passed_along(block, axis, distance):
    devices = range(lax.axis_size(axis))
    route = [((i - distance) % len(devices), i) for i in devices]
    return lax.ppermute(block, axis, route)


def spline_tables():
    cells_line = jnp.arange(NB, dtype=jnp.int32)
    offset = cells_line[:, None] - cells_line[None, :]
    spline = jnp.where(
        offset == 0, 2.0 / 3.0, jnp.where(jnp.abs(offset) == 1, 1.0 / 6.0, 0.0)
    ).astype(jnp.float32)
    second = jnp.where(offset == 0, -2.0, jnp.where(jnp.abs(offset) == 1, 1.0, 0.0)).astype(
        jnp.float32
    )
    plane_value = jnp.einsum("ac,bd->abcd", spline, spline).reshape(NB * NB, NB * NB)
    plane_curve = (
        jnp.einsum("ac,bd->abcd", second, spline) + jnp.einsum("ac,bd->abcd", spline, second)
    ).reshape(NB * NB, NB * NB)
    return (
        spline.astype(jnp.bfloat16),
        second.astype(jnp.bfloat16),
        plane_value.astype(jnp.bfloat16),
        plane_curve.astype(jnp.bfloat16),
    )


def on_device(owned_blips, potential, slot_owner, slot_row, slot_offset):
    spline, second, plane_value, plane_curve = spline_tables()
    domain_count = lax.axis_size("dom")
    slot_count = slot_row.shape[0]
    owned_count = owned_blips.shape[0]
    cell_count = owned_blips.shape[1]
    plane_cells = NB * NB
    capacity = max(2, -(-slot_count // domain_count))
    group_size = domain_count * owned_count
    owner_of = slot_owner[:, 0]
    target = owner_of * owned_count + slot_row
    owner_hot = (owner_of[:, None] == jnp.arange(domain_count, dtype=jnp.int32)[None, :]).astype(
        jnp.int32
    )
    position = jnp.sum(jnp.cumsum(owner_hot, axis=0) * owner_hot, axis=1) - 1
    place_slot = owner_of * capacity + position
    place_hot = place_slot[None, :] == jnp.arange(domain_count * capacity, dtype=jnp.int32)[:, None]
    asked_rows = jnp.sum(jnp.where(place_hot, slot_row[None, :], 0), axis=1) + owned_count * (
        1 - jnp.sum(place_hot.astype(jnp.int32), axis=1)
    )
    place_low = place_hot.astype(jnp.bfloat16)
    gathered_rows = lax.all_gather(owned_blips, "dom", axis=0, tiled=True)
    chosen = (
        target[:, None] == jnp.arange(gathered_rows.shape[0], dtype=jnp.int32)[None, :]
    ).astype(jnp.bfloat16)
    slot_blips = jnp.dot(chosen, gathered_rows, preferred_element_type=jnp.float32).astype(
        jnp.bfloat16
    )
    upper_cells = passed_along(potential, "grp", -1)
    extended = jnp.concatenate([potential[0], upper_cells[0]], axis=0)

    def cut_window(first_row):
        return lax.dynamic_slice_in_dim(extended, first_row, NB, 0)

    window = jax.vmap(cut_window)(slot_offset)
    layered = slot_blips.reshape(slot_count, NB, plane_cells)
    y_value = jnp.einsum("ya,sab->syb", spline, layered, preferred_element_type=jnp.float32).astype(
        jnp.bfloat16
    )
    y_curve = jnp.einsum("ya,sab->syb", second, layered, preferred_element_type=jnp.float32).astype(
        jnp.bfloat16
    )
    flat_value = y_value.reshape(-1, plane_cells)
    values_grid = jnp.dot(flat_value, plane_value, preferred_element_type=jnp.float32)
    laplace = jnp.dot(
        y_curve.reshape(-1, plane_cells), plane_value, preferred_element_type=jnp.float32
    ) + jnp.dot(flat_value, plane_curve, preferred_element_type=jnp.float32)
    applied = (-0.5 * laplace + window.reshape(-1, plane_cells) * values_grid).astype(jnp.bfloat16)
    values_low = values_grid.astype(jnp.bfloat16)
    back_plane = jnp.dot(applied, plane_value, preferred_element_type=jnp.float32).astype(
        jnp.bfloat16
    )
    gradient_piece = jnp.einsum(
        "ay,sab->syb",
        spline,
        back_plane.reshape(slot_count, NB, plane_cells),
        preferred_element_type=jnp.float32,
    ).astype(jnp.bfloat16)
    intersection = lax.dot_general(
        values_low.reshape(slot_count, cell_count),
        applied.reshape(slot_count, cell_count),
        (((1,), (1,)), ((), ())),
        preferred_element_type=jnp.float32,
    ) / float(cell_count)
    select_full = (target[:, None] == jnp.arange(group_size, dtype=jnp.int32)[None, :]).astype(
        jnp.float32
    )
    weighted = jnp.dot(intersection, select_full, precision=lax.Precision.HIGHEST)
    part_hot = (
        target[:, None] == jnp.arange(owned_count * lax.axis_size("dom"), dtype=jnp.int32)[None, :]
    ).astype(jnp.float32)
    hamilton = lax.psum_scatter(
        jnp.dot(part_hot.T, weighted, precision=lax.Precision.HIGHEST),
        "dom",
        scatter_dimension=0,
        tiled=True,
    )
    send_grad = jnp.dot(
        place_low,
        gradient_piece.reshape(slot_count, cell_count),
        preferred_element_type=jnp.bfloat16,
    ).reshape(domain_count, capacity, cell_count)
    got_grad, got_rows = (
        lax.all_to_all(send_grad, "dom", split_axis=0, concat_axis=0, tiled=True),
        lax.all_to_all(
            asked_rows.reshape(domain_count, capacity),
            "dom",
            split_axis=0,
            concat_axis=0,
            tiled=True,
        ),
    )
    owner_pick = (
        got_rows.reshape(-1)[None, :] == jnp.arange(owned_count, dtype=jnp.int32)[:, None]
    ).astype(jnp.bfloat16)
    gradient = jnp.dot(
        owner_pick, got_grad.reshape(-1, cell_count), preferred_element_type=jnp.float32
    )
    return (gradient, hamilton)


def solution(mesh):
    placed = (
        P(("grp", "dom"), None),
        P("dom", "grp", None),
        P(("grp", "dom"), None),
        P(("grp", "dom")),
        P(("grp", "dom")),
    )
    return jax.shard_map(
        on_device,
        mesh=mesh,
        in_specs=placed,
        out_specs=(P(("grp", "dom"), None), P(("grp", "dom"), None)),
        check_vma=False,
    )
```

profile of v0, /device:TPU:0, one launch (start us, length us, event | category | flops | bytes accessed | tf_op | source)
XLA Modules:
  0.0 312.8 jit_solution(663236977083749129)
XLA Ops:
  7.9 0.9 collective-permute-start
  12.6 7.3 %all-to-all-start = ((s32[32,1,2]{2,1,0:T(1,128)}), s32[32,1,2]{2,1,0:T(1,128)S(1)}, u32[]{:S(2)}, u32[]{:S(2)}) async-start(s32[32,1,2]{2,1,0:T(1,128)} %bitcast.1), calls=%async_computation | async-start | bytes 32768 | tf_op jit(solution)/shard_map/all_to_all | solution.py:120
  20.1 7.6 %fusion.1 = (bf16[32,32,32,32]{3,2,1,0:T(8,128)(2,1)}, bf16[32,32,32,32]{3,2,1,0:T(8,128)(2,1)}) fusion(f32[32,32]{1,0:T(8,128)S(1)} %copy.33, f32[32,32]{1,0:T(8,128)S(1)} %copy.30), kind=kLoop, calls=%fused_computation.6 | loop fusion | flops 6291456 | bytes 4202496 | tf_op jit(solution)/shard_map/convert_element_type | solution.py:32
  27.6 12.4 %convert_element_type.78 = bf16[1024,1024]{1,0:T(8,128)(2,1)} reshape(bf16[32,32,32,32]{3,2,1,0:T(8,128)(2,1)} %get-tuple-element.21) | data formatting | bytes 4194304 | tf_op jit(solution)/shard_map/convert_element_type | solution.py:31
  40.1 11.4 %convert_element_type.84 = bf16[1024,1024]{1,0:T(8,128)(2,1)S(1)} reshape(bf16[32,32,32,32]{3,2,1,0:T(8,128)(2,1)} %get-tuple-element.20) | data formatting | bytes 4194304 | tf_op jit(solution)/shard_map/convert_element_type | solution.py:32
  51.5 48.0 %while.1 = (s32[]{:T(128)}, f32[64,1024]{1,0:T(8,128)S(1)}, s32[24,2]{0,1:T(2,128)S(1)}, f32[24,32,1024]{2,1,0:T(8,128)}, s32[]{:T(128)}) while((s32[]{:T(128)}, f32[64,1024]{1,0:T(8,128)S(1)}, s32[24,2]{0,1:T(2,128)S(1)}, f32[24,32,1024]{2,1,0:T(8,128)}, s32[]{:T(128)}) %tuple.24), condition=%wide.while_cond, body=%wide.while_body.sunk | while | flops 2 | bytes 263257 | solution.py:68
  52.2 1.3 bitcast_dynamic-update-slice_fusion.2
  54.2 1.3 bitcast_dynamic-update-slice_fusion.2
  56.2 1.3 bitcast_dynamic-update-slice_fusion.2
  58.2 1.4 bitcast_dynamic-update-slice_fusion.2
  60.2 1.3 bitcast_dynamic-update-slice_fusion.2
  62.2 1.3 bitcast_dynamic-update-slice_fusion.2
  64.2 1.3 bitcast_dynamic-update-slice_fusion.2
  66.2 1.3 bitcast_dynamic-update-slice_fusion.2
  68.2 1.3 bitcast_dynamic-update-slice_fusion.2
  70.2 1.3 bitcast_dynamic-update-slice_fusion.2
  72.2 1.3 bitcast_dynamic-update-slice_fusion.2
  74.2 1.4 bitcast_dynamic-update-slice_fusion.2
  76.2 1.3 bitcast_dynamic-update-slice_fusion.2
  78.2 1.3 bitcast_dynamic-update-slice_fusion.2
  80.2 1.3 bitcast_dynamic-update-slice_fusion.2
  82.2 1.4 bitcast_dynamic-update-slice_fusion.2
  84.2 1.3 bitcast_dynamic-update-slice_fusion.2
  86.2 1.3 bitcast_dynamic-update-slice_fusion.2
  88.2 1.3 bitcast_dynamic-update-slice_fusion.2
  90.2 1.3 bitcast_dynamic-update-slice_fusion.2
  92.1 1.3 bitcast_dynamic-update-slice_fusion.2
  94.1 1.3 bitcast_dynamic-update-slice_fusion.2
  96.1 1.3 bitcast_dynamic-update-slice_fusion.2
  98.1 1.3 bitcast_dynamic-update-slice_fusion.2
  99.5 12.7 %reshape.131 = bf16[128,32768]{1,0:T(8,128)(2,1)} reshape(bf16[32,4,32768]{2,1,0:T(4,128)(2,1)} %all-gather.3.cloned.1.call-done) | data formatting | bytes 16777216
  112.1 4.6 %convolution_convert_fusion = bf16[24,32768]{1,0:T(8,128)(2,1)S(1)} fusion(bf16[128,32768]{1,0:T(8,128)(2,1)} %reshape.131, s32[24]{0:T(128)S(1)} %get-tuple-element.23), kind=kOutput, calls=%fused_computation.2 | convolution fusion | flops 202116096 | bytes 9961568 | tf_op jit(solution)/shard_map/dot_general | solution.py:61
  116.8 0.9 copy.40
  119.0 0.9 copy-done.3
  119.9 3.0 fusion.41
  122.9 1.8 fusion.42
  124.8 1.9 fusion.3
  126.7 1.8 convolution_convert_fusion.4
  129.1 1.0 reshape.135
  130.1 1.4 fusion.5
  131.5 6.3 %copy.35 = bf16[32,2,32768]{2,1,0:T(2,128)(2,1)} copy(bf16[32,2,32768]{2,0,1:T(8,128)(2,1)S(1)} %fusion.5) | data formatting | bytes 8388608 | tf_op jit(solution)/shard_map/dot_general | solution.py:113
  137.8 6.0 %all-to-all-start.1 = ((bf16[32,2,32768]{2,1,0:T(2,128)(2,1)}), bf16[32,2,32768]{2,1,0:T(2,128)(2,1)}, u32[]{:S(2)}, u32[]{:S(2)}) async-start(bf16[32,2,32768]{2,1,0:T(2,128)(2,1)} %copy.35), calls=%async_computation.1 | async-start | bytes 8388608 | tf_op jit(solution)/shard_map/all_to_all | solution.py:119
  144.6 2.6 reshape.109
  148.0 1.0 fusion.8
  150.3 143.6 %all-reduce.4.cloned.1.call-done = f32[128,128]{1,0:T(8,128)} async-done(((f32[128,128]{1,0:T(8,128)}), f32[128,128]{1,0:T(8,128)}) %all-reduce.4.cloned.1.call-update) | async-done | bytes 65552
  293.8 1.3 constant_dynamic-slice_fusion.1
  295.1 7.3 %reshape.108 = bf16[64,32768]{1,0:T(8,128)(2,1)} reshape(bf16[32,2,32768]{2,1,0:T(2,128)(2,1)} %all-to-all-done.1) | data formatting | bytes 8388608 | tf_op jit(solution)/shard_map/reshape | solution.py:132
  302.4 3.6 %fusion.23 = f32[4,32768]{1,0:T(4,128)} fusion(bf16[64,32768]{1,0:T(8,128)(2,1)} %reshape.108, s32[64]{0:T(128)S(1)} %eq.115), kind=kOutput, calls=%fused_computation.45 | convolution fusion | flops 16777472 | bytes 4718848 | tf_op jit(solution)/shard_map/dot_general | solution.py:131
  (92 shorter events, 25.2 us)
Async XLA Ops:
  7.2 92.3 %all-gather.3.cloned.1.call-start = ((), (), s32[]{:S(2)}) async-start(), calls=%async_computation.2 | async-start | bytes 8650752 | tf_op jit(solution)/shard_map/all_gather | solution.py:57
  7.9 43.6 %collective-permute-start = (f32[1,32,1024]{2,1,0:T(8,128)}, f32[1,32,1024]{2,1,0:T(8,128)S(1)}, u32[]{:S(2)}, u32[]{:S(2)}) collective-permute-start(f32[1,32,1024]{2,1,0:T(8,128)} %param.6), channel_id=1, source_target_pairs={{0,0},{1,1},{2,2},{3,3},{4,4},{5,5},{6,6},{7,7},{8,8},{9,9},{10,10... | collective-permute-start | bytes 393224 | tf_op jit(solution)/shard_map/ppermute | solution.py:12
  12.6 125.2 %all-to-all-start = ((s32[32,1,2]{2,1,0:T(1,128)}), s32[32,1,2]{2,1,0:T(1,128)S(1)}, u32[]{:S(2)}, u32[]{:S(2)}) async-start(s32[32,1,2]{2,1,0:T(1,128)} %bitcast.1), calls=%async_computation | async-start | bytes 32768 | tf_op jit(solution)/shard_map/all_to_all | solution.py:120
  20.0 7.6 %copy-start.5 = (s32[24]{0:T(128)S(1)}, s32[24]{0:T(128)}, u32[]{:S(2)}) copy-start(s32[24]{0:T(128)} %param.9) | copy-start | bytes 292
  40.1 11.4 %copy-start.4 = (f32[1,32,1024]{2,1,0:T(8,128)S(1)}, f32[1,32,1024]{2,1,0:T(8,128)}, u32[]{:S(2)}) copy-start(f32[1,32,1024]{2,1,0:T(8,128)} %param.6) | copy-start | bytes 393220
  118.3 1.6 copy-start.3
  122.9 1.9 copy-start.2
  126.7 1.8 copy-start
  137.8 6.0 %copy-start.1 = (bf16[768,1024]{1,0:T(8,128)(2,1)S(1)}, bf16[768,1024]{1,0:T(8,128)(2,1)}, u32[]{:S(2)}) copy-start(bf16[768,1024]{1,0:T(8,128)(2,1)} %copy-done) | copy-start | bytes 4718596
  137.8 157.3 %all-to-all-start.1 = ((bf16[32,2,32768]{2,1,0:T(2,128)(2,1)}), bf16[32,2,32768]{2,1,0:T(2,128)(2,1)}, u32[]{:S(2)}, u32[]{:S(2)}) async-start(bf16[32,2,32768]{2,1,0:T(2,128)(2,1)} %copy.35), calls=%async_computation.1 | async-start | bytes 8388608 | tf_op jit(solution)/shard_map/all_to_all | solution.py:119
  143.7 150.1 %all-reduce.4.cloned.1.call-start = ((), (), s32[]{:S(2)}) async-start(), calls=%async_computation.3 | async-start | bytes 131072
Sparse Core Ops, SparseCore 0:
  10.9 80.1 all-gather.2
  150.7 143.0 all-reduce.3
where the time goes:
time: 316 us; the launch traced here: 313 us
  waiting for transfers between devices  144 us (46%)
  local copies, waits for them, and re-layouts  107 us (34%)
  matrix products  21.8 us (7%)
  between operations  14.3 us (5%)
  starting transfers between devices  14.2 us (4%)
  other arithmetic  11.4 us (4%)
    unnamed x3, waiting for transfers between devices  144 us
    gather x72, local copies, waits for them, and re-layouts  47.9 us
    unnamed x15, local copies, waits for them, and re-layouts  15.8 us
    convert_element_type x1, local copies, waits for them, and re-layouts, spline_tables(): plane_value.astype(jnp.bfloat16)  12.4 us
    convert_element_type x1, local copies, waits for them, and re-layouts, spline_tables(): plane_curve.astype(jnp.bfloat16)  11.4 us
    convert_element_type x1, other arithmetic, spline_tables(): plane_curve.astype(jnp.bfloat16)  7.58 us
    all_to_all x1, starting transfers between devices, on_device(): lax.all_to_all(asked_rows.reshape(domain_count, capacity), 'dom', split_a...  7.3 us
    reshape x1, local copies, waits for them, and re-layouts, on_device(): got_grad.reshape(-1, cell_count)  7.26 us
  transfers between devices with their start and end apart: 5, of which 1 were waited for; matrix products, arithmetic and copies ran while one was open for 41% of the time, Pallas kernels for 0%

commit v1 on v0

v1 whole, which is shorter than its diff:
```python
import functools

import jax
import jax.numpy as jnp
import numpy as np
from jax import lax
from jax.experimental import pallas as pl
from jax.experimental.pallas import tpu as pltpu
from jax.sharding import PartitionSpec as P

NB = 32
HALF = NB // 2
PLANE = NB * NB
VMEM_LIMIT = 56 * 2**20
MESH = pl.DeviceIdType.MESH
HIGHEST = lax.Precision.HIGHEST


def spline_tables():
    cells_line = np.arange(NB, dtype=np.int32)
    offset = cells_line[:, None] - cells_line[None, :]
    spline = np.where(
        offset == 0, 2.0 / 3.0, np.where(np.abs(offset) == 1, 1.0 / 6.0, 0.0)
    ).astype(np.float32)
    second = np.where(offset == 0, -2.0, np.where(np.abs(offset) == 1, 1.0, 0.0)).astype(np.float32)
    plane_value = np.einsum("ac,bd->abcd", spline, spline).reshape(PLANE, PLANE)
    plane_curve = (
        np.einsum("ac,bd->abcd", second, spline) + np.einsum("ac,bd->abcd", spline, second)
    ).reshape(PLANE, PLANE)
    low = jnp.bfloat16
    return spline.astype(low), second.astype(low), plane_value.astype(low), plane_curve.astype(low)


def passed_along(block, axis, distance):
    devices = range(lax.axis_size(axis))
    route = [((i - distance) % len(devices), i) for i in devices]
    return lax.ppermute(block, axis, route)


def digits(index, depth):
    core = index % 2
    a = (index // 2) % 2
    b = (index // 4) % 2
    z = index // 8
    return z, b, a, core


def place(index, depth, order):
    z, b, a, core = digits(index, depth)
    first, second = (a, b) if order == 0 else (b, a)
    return ((core * 2 + first) * 2 + second) * depth + z


def position(depth):
    me = lax.axis_index("dom")
    z, b, a, core = digits(me, depth)
    to_core = me + 1 - 2 * core
    to_a = me + 2 * (1 - 2 * a)
    to_b = me + 4 * (1 - 2 * b)
    along = [lax.rem(z + dz, depth) for dz in range(1, depth)]
    to_z = [me + 8 * (other - z) for other in along]
    return (z, b, a, core), to_core, to_a, to_b, along, to_z


def meet(partners):
    barrier = pltpu.get_barrier_semaphore()
    for partner in partners:
        pl.semaphore_signal(barrier, inc=1, device_id={"dom": partner}, device_id_type=MESH)
    pl.semaphore_wait(barrier, len(partners))


def gather_kernel(depth, rows, own_ref, got_a, got_b, send, recv, local):
    (z, b, a, core), to_core, to_a, to_b, along, to_z = position(depth)
    meet([to_core, to_a, to_b] + to_z)
    got = (got_a, got_b)
    firsts, seconds = (a, b), (b, a)
    to_first, to_second = (to_a, to_b), (to_b, to_a)

    def remote(src, dst, order, row, phase, target):
        return pltpu.make_async_remote_copy(
            src_ref=src,
            dst_ref=dst,
            send_sem=send.at[order, row, phase],
            recv_sem=recv.at[order, row, phase],
            device_id={"dom": target},
            device_id_type=MESH,
        )

    def base(order):
        return ((core * 2 + firsts[order]) * 2 + seconds[order]) * depth

    own, wide = {}, {}
    for row in range(rows):
        for order in range(2):
            piece = own_ref.at[row, pl.ds(order * HALF, HALF)]
            spot = got[order].at[row, base(order) + z]
            for dz in range(1, depth):
                copy = remote(piece, spot, order, row, dz - 1, to_z[dz - 1])
                copy.start()
                wide[order, row, dz - 1] = copy
            copy = pltpu.make_async_copy(piece, spot, local.at[order, row])
            copy.start()
            own[order, row] = copy

    def go(order, row, phase):
        if phase == 0:
            own[order, row].wait()
            for dz in range(1, depth):
                wide[order, row, dz - 1].wait_recv()
            start, size, target = base(order), depth, to_second[order]
        else:
            wide[order, row, depth - 2 + phase].wait_recv()
            if phase == 1:
                start = (core * 2 + firsts[order]) * 2 * depth
                size, target = 2 * depth, to_first[order]
            else:
                start, size, target = core * 4 * depth, 4 * depth, to_core
        block = got[order].at[row, pl.ds(start, size)]
        copy = remote(block, block, order, row, depth - 1 + phase, target)
        copy.start()
        wide[order, row, depth - 1 + phase] = copy

    for step in range(rows + 2):
        for phase in range(3):
            row = step - phase
            if 0 <= row < rows:
                for order in range(2):
                    go(order, row, phase)
    for row in range(rows):
        for order in range(2):
            wide[order, row, depth + 1].wait_recv()
            for phase in range(depth + 2):
                wide[order, row, phase].wait_send()


def gather(own, depth):
    rows = own.shape[0]
    half = jax.ShapeDtypeStruct((rows, 8 * depth, HALF, PLANE), own.dtype)
    return pl.pallas_call(
        functools.partial(gather_kernel, depth, rows),
        out_shape=(half, half),
        in_specs=[pl.BlockSpec(memory_space=pl.ANY)],
        out_specs=[pl.BlockSpec(memory_space=pl.ANY)] * 2,
        scratch_shapes=[
            pltpu.SemaphoreType.DMA((2, rows, depth + 2)),
            pltpu.SemaphoreType.DMA((2, rows, depth + 2)),
            pltpu.SemaphoreType.DMA((2, rows)),
        ],
        compiler_params=pltpu.CompilerParams(collective_id=0, has_side_effects=True),
    )(own)


def domain_kernel(
    group,
    steps,
    place_a,
    place_b,
    row_of,
    offset_of,
    *refs,
):
    blips_a, blips_b = refs[:group], refs[group : 2 * group]
    (field, wide_y, back_y, value_ref, curve_ref, hot_row, hot_column) = refs[2 * group : 2 * group + 7]
    out_a, out_b, out_h, low_ref, applied_ref = refs[2 * group + 7 :]
    step = pl.program_id(0)
    block = group * NB

    @pl.when(step == 0)
    def _():
        zero = jnp.zeros((HALF, PLANE), jnp.bfloat16)
        for row in range(out_a.shape[0]):

            @pl.loop(0, out_a.shape[1])
            def _(spot):
                out_a[row, spot] = zero
                out_b[row, spot] = zero

    blips = jnp.concatenate(
        [half[0, 0] for pair in zip(blips_a, blips_b) for half in pair], axis=0
    )
    both = jnp.dot(wide_y[...], blips, preferred_element_type=jnp.float32).astype(jnp.bfloat16)
    y_value, y_curve = both[:block], both[block:]
    value = value_ref[...]
    values_grid = jnp.dot(y_value, value, preferred_element_type=jnp.float32)
    laplace = jnp.dot(y_curve, value, preferred_element_type=jnp.float32) + jnp.dot(
        y_value, curve_ref[...], preferred_element_type=jnp.float32
    )
    cuts = []
    for k in range(group):
        offset = offset_of[step * group + k]
        near = field[pl.ds(pl.multiple_of(offset // 8 * 8, 8), NB + 8), :]
        cuts.append(pltpu.roll(near, lax.rem(NB + 8 - offset % 8, NB + 8), 0)[:NB])
    window = jnp.concatenate(cuts, axis=0)
    applied = (-0.5 * laplace + window * values_grid).astype(jnp.bfloat16)
    here = pl.ds(pl.multiple_of(step * block, block), block)
    low_ref[here, :] = values_grid.astype(jnp.bfloat16)
    applied_ref[here, :] = applied
    back_plane = jnp.dot(applied, value, preferred_element_type=jnp.float32).astype(jnp.bfloat16)
    piece = jnp.dot(back_y[...], back_plane, preferred_element_type=jnp.float32).astype(
        jnp.bfloat16
    )
    for k in range(group):
        slot = step * group + k
        for out, spot, first in (
            (out_a, place_a[slot], k * NB),
            (out_b, place_b[slot], k * NB + HALF),
        ):
            row = row_of[slot]
            total = out[row, spot].astype(jnp.float32) + piece[first : first + HALF].astype(
                jnp.float32
            )
            out[row, spot] = total.astype(jnp.bfloat16)

    @pl.when(step == steps - 1)
    def _():
        gram = lax.dot_general(
            low_ref[...],
            applied_ref[...],
            (((1,), (1,)), ((), ())),
            preferred_element_type=jnp.float32,
        )
        cell_row = lax.broadcasted_iota(jnp.int32, gram.shape, 0) % NB
        cell_column = lax.broadcasted_iota(jnp.int32, gram.shape, 1) % NB
        terms = jnp.where(cell_row == cell_column, gram, 0.0) / float(NB * PLANE)
        count = gram.shape[0]
        to_column = (
            hot_column[...]
            == lax.broadcasted_iota(jnp.int32, (count, out_h.shape[1]), 1)
        ).astype(jnp.float32)
        to_row = (
            hot_row[...] == lax.broadcasted_iota(jnp.int32, (out_h.shape[0], count), 0)
        ).astype(jnp.float32)
        by_column = jnp.dot(
            terms, to_column, precision=HIGHEST, preferred_element_type=jnp.float32
        )
        out_h[...] = jnp.dot(
            to_row, by_column, precision=HIGHEST, preferred_element_type=jnp.float32
        )


def domain(got_a, got_b, field, owner, row, offset, depth):
    rows, owners = got_a.shape[:2]
    slots = owner.shape[0]
    group = next(g for g in (8, 6, 4, 3, 2, 1) if slots % g == 0)
    steps = slots // group
    spline, second, plane_value, plane_curve = spline_tables()
    eye = np.eye(group, dtype=np.float32)
    spread = lambda table: np.kron(eye, table.astype(np.float32)).astype(jnp.bfloat16)
    wide_y = np.concatenate([spread(spline), spread(second)], axis=0)
    back_y = spread(spline.T)
    place_a, place_b = place(owner, depth, 0), place(owner, depth, 1)
    hot_row = jnp.repeat(place_a * 8 + row, NB)[None, :]
    hot_column = jnp.repeat(owner * rows + row, NB)[:, None]

    def pick(k, which):
        def index(i, at_a, at_b, row_of, offset_of):
            slot = i * group + k
            return (row_of[slot], (at_a if which == 0 else at_b)[slot], 0, 0)

        return pl.BlockSpec((1, 1, HALF, PLANE), index)

    whole = lambda shape: pl.BlockSpec(shape, lambda i, *_: (0,) * len(shape))
    once = lambda shape: pl.BlockSpec(
        shape, lambda i, *_: (0,) * len(shape), pipeline_mode=pl.Buffered(1)
    )
    fixed = (
        field,
        jnp.asarray(wide_y),
        jnp.asarray(back_y),
        jnp.asarray(plane_value),
        jnp.asarray(plane_curve),
        hot_row,
        hot_column,
    )
    dense = jax.ShapeDtypeStruct((rows, owners, HALF, PLANE), jnp.bfloat16)
    flop = 2 * slots * NB * PLANE * PLANE * 4
    return pl.pallas_call(
        functools.partial(domain_kernel, group, steps),
        grid_spec=pltpu.PrefetchScalarGridSpec(
            num_scalar_prefetch=4,
            grid=(steps,),
            in_specs=[pick(k, 0) for k in range(group)]
            + [pick(k, 1) for k in range(group)]
            + [once(x.shape) for x in fixed],
            out_specs=[whole(dense.shape), whole(dense.shape), whole((owners * 8, owners * rows))],
            scratch_shapes=[
                pltpu.VMEM((slots * NB, PLANE), jnp.bfloat16),
                pltpu.VMEM((slots * NB, PLANE), jnp.bfloat16),
            ],
        ),
        out_shape=(
            dense,
            dense,
            jax.ShapeDtypeStruct((owners * 8, owners * rows), jnp.float32),
        ),
        compiler_params=pltpu.CompilerParams(
            vmem_limit_bytes=VMEM_LIMIT, dimension_semantics=("arbitrary",)
        ),
        cost_estimate=pl.CostEstimate(flops=flop, bytes_accessed=2**24, transcendentals=0),
    )(place_a, place_b, row, offset, *([got_a] * group), *([got_b] * group), *fixed)


def scatter_kernel(depth, rows, part_a, part_b, part_h, grad, ham, *scratch):
    (z, b, a, core), to_core, to_a, to_b, along, to_z = position(depth)
    buffers = (scratch[0:4], scratch[4:8], scratch[8:12])
    send, recv = scratch[12:14]
    meet([to_core, to_a, to_b] + to_z)
    parts = (part_a, part_b, part_h)
    firsts, seconds = (a, b, a), (b, a, b)
    to_first, to_second = (to_a, to_b, to_a), (to_b, to_a, to_b)
    flight = {}

    def remote(src, dst, stream, row, phase, target):
        copy = pltpu.make_async_remote_copy(
            src_ref=src,
            dst_ref=dst,
            send_sem=send.at[stream, row, phase],
            recv_sem=recv.at[stream, row, phase],
            device_id={"dom": target},
            device_id_type=MESH,
        )
        copy.start()
        flight[stream, row, phase] = copy

    def add(stream, row, level, source, start, size):
        into = buffers[stream][level]

        @pl.loop(0, size)
        def _(i):
            total = into[row, i].astype(jnp.float32) + source[row, start + i].astype(jnp.float32)
            into[row, i] = total.astype(into.dtype)

    def go(stream, row, phase):
        first, second, zone, last = buffers[stream]
        part = parts[stream]
        if phase == 0:
            remote(
                part.at[row, pl.ds((1 - core) * 4 * depth, 4 * depth)],
                first.at[row], stream, row, 0, to_core,
            )
        elif phase == 1:
            flight[stream, row, 0].wait_recv()
            add(stream, row, 0, part, core * 4 * depth, 4 * depth)
            remote(
                first.at[row, pl.ds((1 - firsts[stream]) * 2 * depth, 2 * depth)],
                second.at[row], stream, row, 1, to_first[stream],
            )
        elif phase == 2:
            flight[stream, row, 1].wait_recv()
            add(stream, row, 1, first, firsts[stream] * 2 * depth, 2 * depth)
            remote(
                second.at[row, pl.ds((1 - seconds[stream]) * depth, depth)],
                zone.at[row], stream, row, 2, to_second[stream],
            )
        elif phase == 3:
            flight[stream, row, 2].wait_recv()
            add(stream, row, 2, second, seconds[stream] * depth, depth)
            for dz in range(1, depth):
                remote(
                    zone.at[row, along[dz - 1]],
                    last.at[row, dz - 1], stream, row, 2 + dz, to_z[dz - 1],
                )
        else:
            for dz in range(1, depth):
                flight[stream, row, 2 + dz].wait_recv()
            total = zone[row, z].astype(jnp.float32)
            for dz in range(1, depth):
                total = total + last[row, dz - 1].astype(jnp.float32)
            if stream == 2:
                ham[...] = total
            else:
                grad[row, stream * HALF : (stream + 1) * HALF, :] = total

    chunks = [[(2, 0), (0, 0), (1, 0)]] + [[(0, row), (1, row)] for row in range(1, rows)]
    for chunk in chunks:
        for stream, row in chunk:
            go(stream, row, 0)
    for step in range(len(chunks) + 3):
        for phase in range(1, 5):
            at = step - (phase - 1)
            if 0 <= at < len(chunks):
                for stream, row in chunks[at]:
                    go(stream, row, phase)
    for copy in flight.values():
        copy.wait_send()


def scatter(part_a, part_b, part_h, depth):
    rows = part_a.shape[0]
    columns = part_h.shape[-1]
    low = lambda count: pltpu.VMEM((rows, count, HALF, PLANE), jnp.bfloat16)
    full = lambda count: pltpu.VMEM((1, count, 8, columns), jnp.float32)
    sizes = (4 * depth, 2 * depth, depth, depth - 1)
    return pl.pallas_call(
        functools.partial(scatter_kernel, depth, rows),
        out_shape=(
            jax.ShapeDtypeStruct((rows, NB, PLANE), jnp.float32),
            jax.ShapeDtypeStruct((8, columns), jnp.float32),
        ),
        in_specs=[pl.BlockSpec(memory_space=pltpu.VMEM)] * 3,
        out_specs=[pl.BlockSpec(memory_space=pltpu.VMEM)] * 2,
        scratch_shapes=[low(n) for n in sizes]
        + [low(n) for n in sizes]
        + [full(n) for n in sizes]
        + [
            pltpu.SemaphoreType.DMA((3, rows, depth + 2)),
            pltpu.SemaphoreType.DMA((3, rows, depth + 2)),
        ],
        compiler_params=pltpu.CompilerParams(
            collective_id=1, has_side_effects=True, vmem_limit_bytes=VMEM_LIMIT
        ),
    )(part_a, part_b, part_h)


def on_device(owned_blips, potential, slot_owner, slot_row, slot_offset):
    devices = lax.axis_size("dom")
    depth = devices // 8
    rows = owned_blips.shape[0]
    owner = slot_owner[:, 0]
    upper = potential if lax.axis_size("grp") == 1 else passed_along(potential, "grp", -1)
    field = jnp.concatenate([potential[0], upper[0]], axis=0)
    got_a, got_b = gather(owned_blips.reshape(rows, NB, PLANE), depth)
    part_a, part_b, part_h = domain(got_a, got_b, field, owner, slot_row, slot_offset, depth)
    grad, ham = scatter(part_a, part_b, part_h.reshape(1, devices, 8, -1), depth)
    return grad.reshape(rows, -1), ham[:rows]


def solution(mesh):
    placed = (
        P(("grp", "dom"), None),
        P("dom", "grp", None),
        P(("grp", "dom"), None),
        P(("grp", "dom")),
        P(("grp", "dom")),
    )
    return jax.shard_map(
        on_device,
        mesh=mesh,
        in_specs=placed,
        out_specs=(P(("grp", "dom"), None), P(("grp", "dom"), None)),
        check_vma=False,
    )
```

time: 316 us -> 150 us (0.47)
  waiting for transfers between devices: 144 us -> 0 us
  Pallas kernels: 0 us -> 138 us
  local copies, waits for them, and re-layouts: 107 us -> 7.11 us
  matrix products: 21.8 us -> 0 us
  starting transfers between devices: 14.2 us -> 0 us
  between operations: 14.3 us -> 0.65 us
  other arithmetic: 11.4 us -> 3.42 us
    unnamed x3 -> x0, waiting for transfers between devices: 144 us -> none
    pallas_call x0 -> x3, Pallas kernels: none -> 138 us  [the longest x1 58.6 us: scatter(): pl.pallas_call(functools.partial(scatter_kernel, depth, rows), out_shape=...]
    gather x72 -> x0, local copies, waits for them, and re-layouts: 47.9 us -> none
    convert_element_type x2 -> x0, local copies, waits for them, and re-layouts: 23.8 us -> none  [the longest x1 12.4 us: spline_tables(): plane_value.astype(jnp.bfloat16)]
    dot_general x13 -> x0, matrix products: 21.8 us -> none  [the longest x1 4.62 us: on_device(): jnp.dot(chosen, gathered_rows, preferred_element_type=jnp.float32)]
    all_to_all x2 -> x0, starting transfers between devices: 13.3 us -> none  [the longest x1 7.3 us: on_device(): lax.all_to_all(asked_rows.reshape(domain_count, capacity), 'dom', split_a...]
    unnamed x15 -> x2, local copies, waits for them, and re-layouts: 15.8 us -> 3.9 us
    reshape x4 -> x0, local copies, waits for them, and re-layouts: 11.6 us -> none  [the longest x1 7.26 us: on_device(): got_grad.reshape(-1, cell_count)]
  transfers between devices with their start and end apart: 5 -> 0, of which waited for: 1 -> 0; matrix products, arithmetic and copies ran while one was open for 41% -> 0% of each run, Pallas kernels for 0% -> 0%
where the time goes in v1:
time: 150 us; the launch traced here: 149 us
  Pallas kernels  138 us (92%)
  local copies, waits for them, and re-layouts  7.11 us (5%)
  other arithmetic  3.42 us (2%)
    pallas_call x1, Pallas kernels, scatter(): pl.pallas_call(functools.partial(scatter_kernel, depth, rows), out_shape=...  58.6 us
    pallas_call x1, Pallas kernels, gather(): pl.pallas_call(functools.partial(gather_kernel, depth, rows), out_shape=(...  56.4 us
    pallas_call x1, Pallas kernels, domain(): pl.pallas_call(functools.partial(domain_kernel, group, steps), grid_spec=...  23 us
    unnamed x2, local copies, waits for them, and re-layouts  3.9 us

profile of v1, /device:TPU:0, one launch (start us, length us, event | category | flops | bytes accessed | tf_op | source)
XLA Modules:
  0.0 149.3 jit_solution(12259067743905005458)
XLA Ops:
  0.6 1.2 multiply_add_fusion
  1.8 0.5 multiply_add_fusion.1.place_b
  2.4 0.1 broadcast_in_dim.6
  2.4 0.7 broadcast_in_dim_reshape.6.refs_21_
  3.1 0.1 broadcast_in_dim.7
  3.2 1.7 %copy.15 = bf16[1,4,32,1024]{3,2,1,0:T(8,128)(2,1)} copy(bf16[1,4,32,1024]{3,1,2,0:T(4,128)(2,1)} %bitcast.48) | data formatting | bytes 524288
  4.9 1.7 %pad_maximum_fusion.refs_16_ = f32[64,1024]{1,0:T(8,128)} fusion(f32[32,1024]{1,0:T(8,128)} %bitcast.50), kind=kLoop, calls=%fused_computation.1 | loop fusion | flops 65536 | bytes 393216 | tf_op jit(solution)/shard_map/concatenate | solution.py:421
  6.6 1.1 broadcast_in_dim_reshape.8.refs_22_
  7.7 56.4 %shard_map.104 = (bf16[4,32,16,1024]{3,2,1,0:T(8,128)(2,1)}, bf16[4,32,16,1024]{3,2,1,0:T(8,128)(2,1)}) custom-call(bf16[4,32,1024]{2,1,0:T(8,128)(2,1)} %bitcast.45), custom_call_target="tpu_custom_call" | custom-call | tf_op jit(solution)/shard_map/pallas_call | solution.py:139
  64.2 23.0 %shard_map.105 = (bf16[4,32,16,1024]{3,2,1,0:T(8,128)(2,1)}, bf16[4,32,16,1024]{3,2,1,0:T(8,128)(2,1)}, f32[256,128]{1,0:T(8,128)}) custom-call(s32[24]{0:T(128)} %get-tuple-element.17.place_a, s32[24]{0:T(128)} %multiply_add_fusion.1.place_b, s32[24]{0:T(128)} %row_of.1, s32[24]{0:T(128)} %offset_of.1, ...), custom_call_target="tpu_custom_call" | custom-call | flops 6442450944 | bytes 16777216 | tf_op jit(solution)/shard_map/pallas_call | solution.py:277
  87.2 58.6 %shard_map.106 = (f32[4,32,1024]{2,1,0:T(8,128)}, f32[8,128]{1,0:T(8,128)}) custom-call(bf16[4,32,16,1024]{3,2,1,0:T(8,128)(2,1)} %get-tuple-element.11.part_a, bf16[4,32,16,1024]{3,2,1,0:T(8,128)(2,1)} %get-tuple-element.12.part_b, f32[1,32,8,128]{3,2,1,0:T(8,128)} %bitcast.49), custom_call_target="tpu_custom_call" | custom-call | tf_op jit(solution)/shard_map/pallas_call | solution.py:394
  145.8 2.2 %copy.13 = f32[1,4,32,1024]{3,1,2,0:T(4,128)} copy(f32[1,4,32,1024]{3,2,1,0:T(8,128)} %bitcast.47) | data formatting | bytes 1048576
  148.0 1.3 slice.3

commit v2 on v1

--- a/solution.py
+++ b/solution.py
@@ -90,7 +90,8 @@
         return ((core * 2 + firsts[order]) * 2 + seconds[order]) * depth
 
     own, wide = {}, {}
-    for row in range(rows):
+
+    def begin(row):
         for order in range(2):
             piece = own_ref.at[row, pl.ds(order * HALF, HALF)]
             spot = got[order].at[row, base(order) + z]
@@ -104,6 +105,8 @@
 
     def go(order, row, phase):
         if phase == 0:
+            if order == 0 and row + 1 < rows:
+                begin(row + 1)
             own[order, row].wait()
             for dz in range(1, depth):
                 wide[order, row, dz - 1].wait_recv()
@@ -120,6 +123,7 @@
         copy.start()
         wide[order, row, depth - 1 + phase] = copy
 
+    begin(0)
     for step in range(rows + 2):
         for phase in range(3):
             row = step - phase
@@ -153,20 +157,23 @@
 def domain_kernel(
     group,
     steps,
-    place_a,
-    place_b,
+    depth,
+    owner_of,
     row_of,
     offset_of,
     *refs,
 ):
     blips_a, blips_b = refs[:group], refs[group : 2 * group]
-    (field, wide_y, back_y, value_ref, curve_ref, hot_row, hot_column) = refs[2 * group : 2 * group + 7]
-    out_a, out_b, out_h, low_ref, applied_ref = refs[2 * group + 7 :]
+    (lower, upper, wide_y, back_y, value_ref, curve_ref) = refs[2 * group : 2 * group + 6]
+    out_a, out_b, out_h, low_ref, applied_ref, field = refs[2 * group + 6 :]
     step = pl.program_id(0)
     block = group * NB
 
     @pl.when(step == 0)
     def _():
+        count = lower.shape[0]
+        field[:count] = lower[...]
+        field[count:] = upper[...]
         zero = jnp.zeros((HALF, PLANE), jnp.bfloat16)
         for row in range(out_a.shape[0]):
 
@@ -201,10 +208,8 @@
     )
     for k in range(group):
         slot = step * group + k
-        for out, spot, first in (
-            (out_a, place_a[slot], k * NB),
-            (out_b, place_b[slot], k * NB + HALF),
-        ):
+        for out, order, first in ((out_a, 0, k * NB), (out_b, 1, k * NB + HALF)):
+            spot = place(owner_of[slot, 0], depth, order)
             row = row_of[slot]
             total = out[row, spot].astype(jnp.float32) + piece[first : first + HALF].astype(
                 jnp.float32
@@ -223,22 +228,31 @@
         cell_column = lax.broadcasted_iota(jnp.int32, gram.shape, 1) % NB
         terms = jnp.where(cell_row == cell_column, gram, 0.0) / float(NB * PLANE)
         count = gram.shape[0]
+        slot = lax.broadcasted_iota(jnp.int32, (1, count), 1) // NB
+        hot_row, hot_column = jnp.zeros_like(slot), jnp.zeros_like(slot)
+        for k in range(count // NB):
+            owner, row = owner_of[k, 0], row_of[k]
+            hot_row = jnp.where(slot == k, place(owner, depth, 0) * 8 + row, hot_row)
+            hot_column = jnp.where(slot == k, owner * out_a.shape[0] + row, hot_column)
         to_column = (
-            hot_column[...]
-            == lax.broadcasted_iota(jnp.int32, (count, out_h.shape[1]), 1)
+            hot_column == lax.broadcasted_iota(jnp.int32, (out_h.shape[1], count), 0)
         ).astype(jnp.float32)
         to_row = (
-            hot_row[...] == lax.broadcasted_iota(jnp.int32, (out_h.shape[0], count), 0)
+            hot_row == lax.broadcasted_iota(jnp.int32, (out_h.shape[0], count), 0)
         ).astype(jnp.float32)
-        by_column = jnp.dot(
-            terms, to_column, precision=HIGHEST, preferred_element_type=jnp.float32
+        by_column = lax.dot_general(
+            terms,
+            to_column,
+            (((1,), (1,)), ((), ())),
+            precision=HIGHEST,
+            preferred_element_type=jnp.float32,
         )
         out_h[...] = jnp.dot(
             to_row, by_column, precision=HIGHEST, preferred_element_type=jnp.float32
         )
 
 
-def domain(got_a, got_b, field, owner, row, offset, depth):
+def domain(got_a, got_b, lower, upper, owner, row, offset, depth):
     rows, owners = got_a.shape[:2]
     slots = owner.shape[0]
     group = next(g for g in (8, 6, 4, 3, 2, 1) if slots % g == 0)
@@ -248,14 +262,11 @@
     spread = lambda table: np.kron(eye, table.astype(np.float32)).astype(jnp.bfloat16)
     wide_y = np.concatenate([spread(spline), spread(second)], axis=0)
     back_y = spread(spline.T)
-    place_a, place_b = place(owner, depth, 0), place(owner, depth, 1)
-    hot_row = jnp.repeat(place_a * 8 + row, NB)[None, :]
-    hot_column = jnp.repeat(owner * rows + row, NB)[:, None]
 
     def pick(k, which):
-        def index(i, at_a, at_b, row_of, offset_of):
+        def index(i, owner_of, row_of, offset_of):
             slot = i * group + k
-            return (row_of[slot], (at_a if which == 0 else at_b)[slot], 0, 0)
+            return (row_of[slot], place(owner_of[slot, 0], depth, which), 0, 0)
 
         return pl.BlockSpec((1, 1, HALF, PLANE), index)
 
@@ -264,20 +275,19 @@
         shape, lambda i, *_: (0,) * len(shape), pipeline_mode=pl.Buffered(1)
     )
     fixed = (
-        field,
+        lower,
+        upper,
         jnp.asarray(wide_y),
         jnp.asarray(back_y),
         jnp.asarray(plane_value),
         jnp.asarray(plane_curve),
-        hot_row,
-        hot_column,
     )
     dense = jax.ShapeDtypeStruct((rows, owners, HALF, PLANE), jnp.bfloat16)
     flop = 2 * slots * NB * PLANE * PLANE * 4
     return pl.pallas_call(
-        functools.partial(domain_kernel, group, steps),
+        functools.partial(domain_kernel, group, steps, depth),
         grid_spec=pltpu.PrefetchScalarGridSpec(
-            num_scalar_prefetch=4,
+            num_scalar_prefetch=3,
             grid=(steps,),
             in_specs=[pick(k, 0) for k in range(group)]
             + [pick(k, 1) for k in range(group)]
@@ -286,6 +296,7 @@
             scratch_shapes=[
                 pltpu.VMEM((slots * NB, PLANE), jnp.bfloat16),
                 pltpu.VMEM((slots * NB, PLANE), jnp.bfloat16),
+                pltpu.VMEM((2 * lower.shape[0], PLANE), jnp.float32),
             ],
         ),
         out_shape=(
@@ -297,13 +308,24 @@
             vmem_limit_bytes=VMEM_LIMIT, dimension_semantics=("arbitrary",)
         ),
         cost_estimate=pl.CostEstimate(flops=flop, bytes_accessed=2**24, transcendentals=0),
-    )(place_a, place_b, row, offset, *([got_a] * group), *([got_b] * group), *fixed)
+    )(owner, row, offset, *([got_a] * group), *([got_b] * group), *fixed)
 
 
 def scatter_kernel(depth, rows, part_a, part_b, part_h, grad, ham, *scratch):
     (z, b, a, core), to_core, to_a, to_b, along, to_z = position(depth)
     buffers = (scratch[0:4], scratch[4:8], scratch[8:12])
-    send, recv = scratch[12:14]
+    send, recv, local = scratch[12:15]
+    mine = scratch[15:17]
+    held = {}
+    for row in range(rows):
+        for stream, part in enumerate((part_a, part_b)):
+            copy = pltpu.make_async_copy(
+                part.at[row, pl.ds(core * 4 * depth, 4 * depth)],
+                mine[stream].at[row],
+                local.at[stream, row],
+            )
+            copy.start()
+            held[stream, row] = copy
     meet([to_core, to_a, to_b] + to_z)
     parts = (part_a, part_b, part_h)
     firsts, seconds = (a, b, a), (b, a, b)
@@ -325,10 +347,9 @@
     def add(stream, row, level, source, start, size):
         into = buffers[stream][level]
 
-        @pl.loop(0, size)
+        @pl.loop(0, size, unroll=2)
         def _(i):
-            total = into[row, i].astype(jnp.float32) + source[row, start + i].astype(jnp.float32)
-            into[row, i] = total.astype(into.dtype)
+            into[row, i] = into[row, i] + source[row, start + i]
 
     def go(stream, row, phase):
         first, second, zone, last = buffers[stream]
@@ -340,7 +361,11 @@
             )
         elif phase == 1:
             flight[stream, row, 0].wait_recv()
-            add(stream, row, 0, part, core * 4 * depth, 4 * depth)
+            if stream == 2:
+                add(stream, row, 0, part, core * 4 * depth, 4 * depth)
+            else:
+                held[stream, row].wait()
+                add(stream, row, 0, mine[stream], 0, 4 * depth)
             remote(
                 first.at[row, pl.ds((1 - firsts[stream]) * 2 * depth, 2 * depth)],
                 second.at[row], stream, row, 1, to_first[stream],
@@ -397,7 +422,8 @@
             jax.ShapeDtypeStruct((rows, NB, PLANE), jnp.float32),
             jax.ShapeDtypeStruct((8, columns), jnp.float32),
         ),
-        in_specs=[pl.BlockSpec(memory_space=pltpu.VMEM)] * 3,
+        in_specs=[pl.BlockSpec(memory_space=pl.ANY)] * 2
+        + [pl.BlockSpec(memory_space=pltpu.VMEM)],
         out_specs=[pl.BlockSpec(memory_space=pltpu.VMEM)] * 2,
         scratch_shapes=[low(n) for n in sizes]
         + [low(n) for n in sizes]
@@ -405,7 +431,9 @@
         + [
             pltpu.SemaphoreType.DMA((3, rows, depth + 2)),
             pltpu.SemaphoreType.DMA((3, rows, depth + 2)),
-        ],
+            pltpu.SemaphoreType.DMA((2, rows)),
+        ]
+        + [low(sizes[0])] * 2,
         compiler_params=pltpu.CompilerParams(
             collective_id=1, has_side_effects=True, vmem_limit_bytes=VMEM_LIMIT
         ),
@@ -416,11 +444,11 @@
     devices = lax.axis_size("dom")
     depth = devices // 8
     rows = owned_blips.shape[0]
-    owner = slot_owner[:, 0]
     upper = potential if lax.axis_size("grp") == 1 else passed_along(potential, "grp", -1)
-    field = jnp.concatenate([potential[0], upper[0]], axis=0)
     got_a, got_b = gather(owned_blips.reshape(rows, NB, PLANE), depth)
-    part_a, part_b, part_h = domain(got_a, got_b, field, owner, slot_row, slot_offset, depth)
+    part_a, part_b, part_h = domain(
+        got_a, got_b, potential[0], upper[0], slot_owner, slot_row, slot_offset, depth
+    )
     grad, ham = scatter(part_a, part_b, part_h.reshape(1, devices, 8, -1), depth)
     return grad.reshape(rows, -1), ham[:rows]
 

time: 150 us -> 145 us (0.967)
  other arithmetic: 3.42 us -> 0 us
    pallas_call x1, Pallas kernels: 23 us -> 26.6 us  [domain(): pl.pallas_call(functools.partial(domain_kernel, group, steps, depth), gri...]
    pallas_call x1, Pallas kernels: 56.4 us -> 53.8 us  [gather(): pl.pallas_call(functools.partial(gather_kernel, depth, rows), out_shape=(...]
    another operation x2 -> x0, local copies, waits for them, and re-layouts: 1.82 us -> none  [the longest x1 1.14 us: domain(): hot_column = jnp.repeat(owner * rows + row, NB)[:, None]]
    add x2 -> x0, other arithmetic: 1.73 us -> none  [the longest x1 1.21 us: domain(): hot_row = jnp.repeat(place_a * 8 + row, NB)[None, :]]
    concatenate x1 -> x0, other arithmetic: 1.69 us -> none  [on_device(): field = jnp.concatenate([potential[0], upper[0]], axis=0)]
    unnamed x2 -> x3, local copies, waits for them, and re-layouts: 3.9 us -> 5.24 us
where the time goes in v2:
time: 145 us
  Pallas kernels  138 us (95%)
  local copies, waits for them, and re-layouts  6.49 us (4%)
    pallas_call x1, Pallas kernels, scatter(): pl.pallas_call(functools.partial(scatter_kernel, depth, rows), out_shape=...  57.6 us
    pallas_call x1, Pallas kernels, gather(): pl.pallas_call(functools.partial(gather_kernel, depth, rows), out_shape=(...  53.8 us
    pallas_call x1, Pallas kernels, domain(): pl.pallas_call(functools.partial(domain_kernel, group, steps, depth), gri...  26.6 us
    unnamed x3, local copies, waits for them, and re-layouts  5.24 us

profile of v2, /device:TPU:0, one launch (start us, length us, event | category | flops | bytes accessed | tf_op | source)
XLA Modules:
  0.0 145.2 jit_solution(11901291219919193610)
XLA Ops:
  0.6 1.3 copy.11.owner_of
  2.0 1.7 %copy.15 = bf16[1,4,32,1024]{3,2,1,0:T(8,128)(2,1)} copy(bf16[1,4,32,1024]{3,1,2,0:T(4,128)(2,1)} %bitcast.13) | data formatting | bytes 524288
  3.7 53.8 %shard_map.104 = (bf16[4,32,16,1024]{3,2,1,0:T(8,128)(2,1)}, bf16[4,32,16,1024]{3,2,1,0:T(8,128)(2,1)}) custom-call(bf16[4,32,1024]{2,1,0:T(8,128)(2,1)} %bitcast.8), custom_call_target="tpu_custom_call" | custom-call | tf_op jit(solution)/shard_map/pallas_call | solution.py:143
  57.5 26.6 %shard_map.105 = (bf16[4,32,16,1024]{3,2,1,0:T(8,128)(2,1)}, bf16[4,32,16,1024]{3,2,1,0:T(8,128)(2,1)}, f32[256,128]{1,0:T(8,128)}) custom-call(s32[24,1]{1,0:T(8,128)} %copy.11.owner_of, s32[24]{0:T(128)} %row_of.1, s32[24]{0:T(128)} %offset_of.1, bf16[4,32,16,1024]{3,2,1,0:T(8,128)(2,1)} %get-tuple-element.9.refs_0_.refs_1_.refs_2_.refs_3_.refs_4_.refs_5_.refs_6_.refs_7_, ...), custom_call_target="tpu_custom_call" | custom-call | flops 6442450944 | bytes 16777216 | tf_op jit(solution)/shard_map/pallas_call | solution.py:287
  84.1 57.6 %shard_map.106 = (f32[4,32,1024]{2,1,0:T(8,128)}, f32[8,128]{1,0:T(8,128)}) custom-call(bf16[4,32,16,1024]{3,2,1,0:T(8,128)(2,1)} %get-tuple-element.11.part_a, bf16[4,32,16,1024]{3,2,1,0:T(8,128)(2,1)} %get-tuple-element.12.part_b, f32[1,32,8,128]{3,2,1,0:T(8,128)} %bitcast.14), custom_call_target="tpu_custom_call" | custom-call | tf_op jit(solution)/shard_map/pallas_call | solution.py:419
  141.7 2.2 %copy.13 = f32[1,4,32,1024]{3,1,2,0:T(4,128)} copy(f32[1,4,32,1024]{3,2,1,0:T(8,128)} %bitcast.12) | data formatting | bytes 1048576
  143.9 1.2 slice.3

commit v3 on v2

--- a/solution.py
+++ b/solution.py
@@ -46,9 +46,9 @@
 
 
 def place(index, depth, order):
-    z, b, a, core = digits(index, depth)
+    core, a, b, z = index & 1, (index >> 1) & 1, (index >> 2) & 1, index >> 3
     first, second = (a, b) if order == 0 else (b, a)
-    return ((core * 2 + first) * 2 + second) * depth + z
+    return ((core << 2) + (first << 1) + second) * depth + z
 
 
 def position(depth):
@@ -195,8 +195,9 @@
     cuts = []
     for k in range(group):
         offset = offset_of[step * group + k]
-        near = field[pl.ds(pl.multiple_of(offset // 8 * 8, 8), NB + 8), :]
-        cuts.append(pltpu.roll(near, lax.rem(NB + 8 - offset % 8, NB + 8), 0)[:NB])
+        low_bits = offset & 7
+        near = field[pl.ds(pl.multiple_of(offset - low_bits, 8), NB + 8), :]
+        cuts.append(pltpu.roll(near, jnp.where(low_bits == 0, 0, NB + 8 - low_bits), 0)[:NB])
     window = jnp.concatenate(cuts, axis=0)
     applied = (-0.5 * laplace + window * values_grid).astype(jnp.bfloat16)
     here = pl.ds(pl.multiple_of(step * block, block), block)
@@ -224,8 +225,8 @@
             (((1,), (1,)), ((), ())),
             preferred_element_type=jnp.float32,
         )
-        cell_row = lax.broadcasted_iota(jnp.int32, gram.shape, 0) % NB
-        cell_column = lax.broadcasted_iota(jnp.int32, gram.shape, 1) % NB
+        cell_row = lax.broadcasted_iota(jnp.int32, gram.shape, 0) & (NB - 1)
+        cell_column = lax.broadcasted_iota(jnp.int32, gram.shape, 1) & (NB - 1)
         terms = jnp.where(cell_row == cell_column, gram, 0.0) / float(NB * PLANE)
         count = gram.shape[0]
         slot = lax.broadcasted_iota(jnp.int32, (1, count), 1) // NB

time: 145 us -> 143 us (0.986)
  Pallas kernels: 138 us -> 135 us
    pallas_call x1, Pallas kernels: 26.6 us -> 23.9 us  [domain(): pl.pallas_call(functools.partial(domain_kernel, group, steps, depth), gri...]
where the time goes in v3:
time: 143 us; the launch traced here: 142 us
  Pallas kernels  135 us (94%)
  local copies, waits for them, and re-layouts  6.49 us (5%)
    pallas_call x1, Pallas kernels, scatter(): pl.pallas_call(functools.partial(scatter_kernel, depth, rows), out_shape=...  57.6 us
    pallas_call x1, Pallas kernels, gather(): pl.pallas_call(functools.partial(gather_kernel, depth, rows), out_shape=(...  53.8 us
    pallas_call x1, Pallas kernels, domain(): pl.pallas_call(functools.partial(domain_kernel, group, steps, depth), gri...  23.9 us
    unnamed x3, local copies, waits for them, and re-layouts  5.24 us

profile of v3, /device:TPU:0, one launch (start us, length us, event | category | flops | bytes accessed | tf_op | source)
XLA Modules:
  0.0 142.5 jit_solution(14782769261826287768)
XLA Ops:
  0.6 1.3 copy.11.owner_of
  2.0 1.7 %copy.15 = bf16[1,4,32,1024]{3,2,1,0:T(8,128)(2,1)} copy(bf16[1,4,32,1024]{3,1,2,0:T(4,128)(2,1)} %bitcast.13) | data formatting | bytes 524288
  3.7 53.8 %shard_map.104 = (bf16[4,32,16,1024]{3,2,1,0:T(8,128)(2,1)}, bf16[4,32,16,1024]{3,2,1,0:T(8,128)(2,1)}) custom-call(bf16[4,32,1024]{2,1,0:T(8,128)(2,1)} %bitcast.8), custom_call_target="tpu_custom_call" | custom-call | tf_op jit(solution)/shard_map/pallas_call | solution.py:143
  57.5 23.9 %shard_map.105 = (bf16[4,32,16,1024]{3,2,1,0:T(8,128)(2,1)}, bf16[4,32,16,1024]{3,2,1,0:T(8,128)(2,1)}, f32[256,128]{1,0:T(8,128)}) custom-call(s32[24,1]{1,0:T(8,128)} %copy.11.owner_of, s32[24]{0:T(128)} %row_of.1, s32[24]{0:T(128)} %offset_of.1, bf16[4,32,16,1024]{3,2,1,0:T(8,128)(2,1)} %get-tuple-element.9.refs_0_.refs_1_.refs_2_.refs_3_.refs_4_.refs_5_.refs_6_.refs_7_, ...), custom_call_target="tpu_custom_call" | custom-call | flops 6442450944 | bytes 16777216 | tf_op jit(solution)/shard_map/pallas_call | solution.py:288
  81.4 57.6 %shard_map.106 = (f32[4,32,1024]{2,1,0:T(8,128)}, f32[8,128]{1,0:T(8,128)}) custom-call(bf16[4,32,16,1024]{3,2,1,0:T(8,128)(2,1)} %get-tuple-element.11.part_a, bf16[4,32,16,1024]{3,2,1,0:T(8,128)(2,1)} %get-tuple-element.12.part_b, f32[1,32,8,128]{3,2,1,0:T(8,128)} %bitcast.14), custom_call_target="tpu_custom_call" | custom-call | tf_op jit(solution)/shard_map/pallas_call | solution.py:420
  139.0 2.2 %copy.13 = f32[1,4,32,1024]{3,1,2,0:T(4,128)} copy(f32[1,4,32,1024]{3,2,1,0:T(8,128)} %bitcast.12) | data formatting | bytes 1048576
  141.2 1.2 slice.3

commit v4 on v3

--- a/solution.py
+++ b/solution.py
@@ -13,7 +13,6 @@
 PLANE = NB * NB
 VMEM_LIMIT = 56 * 2**20
 MESH = pl.DeviceIdType.MESH
-HIGHEST = lax.Precision.HIGHEST
 
 
 def spline_tables():
@@ -154,6 +153,13 @@
     )(own)
 
 
+def split(wide):
+    high = wide.astype(jnp.bfloat16)
+    rest = wide - high.astype(jnp.float32)
+    middle = rest.astype(jnp.bfloat16)
+    return high, middle, (rest - middle.astype(jnp.float32)).astype(jnp.bfloat16)
+
+
 def domain_kernel(
     group,
     steps,
@@ -177,7 +183,7 @@
         zero = jnp.zeros((HALF, PLANE), jnp.bfloat16)
         for row in range(out_a.shape[0]):
 
-            @pl.loop(0, out_a.shape[1])
+            @pl.loop(0, out_a.shape[1], unroll=4)
             def _(spot):
                 out_a[row, spot] = zero
                 out_b[row, spot] = zero
@@ -235,22 +241,21 @@
             owner, row = owner_of[k, 0], row_of[k]
             hot_row = jnp.where(slot == k, place(owner, depth, 0) * 8 + row, hot_row)
             hot_column = jnp.where(slot == k, owner * out_a.shape[0] + row, hot_column)
-        to_column = (
-            hot_column == lax.broadcasted_iota(jnp.int32, (out_h.shape[1], count), 0)
-        ).astype(jnp.float32)
-        to_row = (
-            hot_row == lax.broadcasted_iota(jnp.int32, (out_h.shape[0], count), 0)
-        ).astype(jnp.float32)
-        by_column = lax.dot_general(
-            terms,
-            to_column,
-            (((1,), (1,)), ((), ())),
-            precision=HIGHEST,
-            preferred_element_type=jnp.float32,
-        )
-        out_h[...] = jnp.dot(
-            to_row, by_column, precision=HIGHEST, preferred_element_type=jnp.float32
-        )
+        to_column = jnp.where(
+            hot_column == lax.broadcasted_iota(jnp.int32, (out_h.shape[1], count), 0), 1.0, 0.0
+        ).astype(jnp.bfloat16)
+        to_row = jnp.where(
+            hot_row == lax.broadcasted_iota(jnp.int32, (out_h.shape[0], count), 0), 1.0, 0.0
+        ).astype(jnp.bfloat16)
+        by_column = 0.0
+        for part in split(terms):
+            by_column += lax.dot_general(
+                part, to_column, (((1,), (1,)), ((), ())), preferred_element_type=jnp.float32
+            )
+        total = 0.0
+        for part in split(by_column):
+            total += jnp.dot(to_row, part, preferred_element_type=jnp.float32)
+        out_h[...] = total
 
 
 def domain(got_a, got_b, lower, upper, owner, row, offset, depth):

time: 143 us -> 141 us (0.986)
  Pallas kernels: 135 us -> 133 us
    pallas_call x1, Pallas kernels: 23.9 us -> 21.9 us  [domain(): pl.pallas_call(functools.partial(domain_kernel, group, steps, depth), gri...]
where the time goes in v4:
time: 141 us; the launch traced here: 140 us
  Pallas kernels  133 us (94%)
  local copies, waits for them, and re-layouts  6.49 us (5%)
    pallas_call x1, Pallas kernels, scatter(): pl.pallas_call(functools.partial(scatter_kernel, depth, rows), out_shape=...  57.6 us
    pallas_call x1, Pallas kernels, gather(): pl.pallas_call(functools.partial(gather_kernel, depth, rows), out_shape=(...  53.8 us
    pallas_call x1, Pallas kernels, domain(): pl.pallas_call(functools.partial(domain_kernel, group, steps, depth), gri...  21.9 us
    unnamed x3, local copies, waits for them, and re-layouts  5.24 us

profile of v4, /device:TPU:0, one launch (start us, length us, event | category | flops | bytes accessed | tf_op | source)
XLA Modules:
  0.0 140.4 jit_solution(8228447525512717107)
XLA Ops:
  0.6 1.3 copy.11.owner_of
  2.0 1.7 %copy.15 = bf16[1,4,32,1024]{3,2,1,0:T(8,128)(2,1)} copy(bf16[1,4,32,1024]{3,1,2,0:T(4,128)(2,1)} %bitcast.13) | data formatting | bytes 524288
  3.7 53.8 %shard_map.104 = (bf16[4,32,16,1024]{3,2,1,0:T(8,128)(2,1)}, bf16[4,32,16,1024]{3,2,1,0:T(8,128)(2,1)}) custom-call(bf16[4,32,1024]{2,1,0:T(8,128)(2,1)} %bitcast.8), custom_call_target="tpu_custom_call" | custom-call | tf_op jit(solution)/shard_map/pallas_call | solution.py:142
  57.5 21.9 %shard_map.105 = (bf16[4,32,16,1024]{3,2,1,0:T(8,128)(2,1)}, bf16[4,32,16,1024]{3,2,1,0:T(8,128)(2,1)}, f32[256,128]{1,0:T(8,128)}) custom-call(s32[24,1]{1,0:T(8,128)} %copy.11.owner_of, s32[24]{0:T(128)} %row_of.1, s32[24]{0:T(128)} %offset_of.1, bf16[4,32,16,1024]{3,2,1,0:T(8,128)(2,1)} %get-tuple-element.9.refs_0_.refs_1_.refs_2_.refs_3_.refs_4_.refs_5_.refs_6_.refs_7_, ...), custom_call_target="tpu_custom_call" | custom-call | flops 6442450944 | bytes 16777216 | tf_op jit(solution)/shard_map/pallas_call | solution.py:293
  79.4 57.6 %shard_map.106 = (f32[4,32,1024]{2,1,0:T(8,128)}, f32[8,128]{1,0:T(8,128)}) custom-call(bf16[4,32,16,1024]{3,2,1,0:T(8,128)(2,1)} %get-tuple-element.11.part_a, bf16[4,32,16,1024]{3,2,1,0:T(8,128)(2,1)} %get-tuple-element.12.part_b, f32[1,32,8,128]{3,2,1,0:T(8,128)} %bitcast.14), custom_call_target="tpu_custom_call" | custom-call | tf_op jit(solution)/shard_map/pallas_call | solution.py:425
  137.0 2.2 %copy.13 = f32[1,4,32,1024]{3,1,2,0:T(4,128)} copy(f32[1,4,32,1024]{3,2,1,0:T(8,128)} %bitcast.12) | data formatting | bytes 1048576
  139.2 1.2 slice.3

commit v5 on v4

--- a/solution.py
+++ b/solution.py
@@ -216,7 +216,7 @@
     for k in range(group):
         slot = step * group + k
         for out, order, first in ((out_a, 0, k * NB), (out_b, 1, k * NB + HALF)):
-            spot = place(owner_of[slot, 0], depth, order)
+            spot = place(owner_of[slot], depth, order)
             row = row_of[slot]
             total = out[row, spot].astype(jnp.float32) + piece[first : first + HALF].astype(
                 jnp.float32
@@ -238,7 +238,7 @@
         slot = lax.broadcasted_iota(jnp.int32, (1, count), 1) // NB
         hot_row, hot_column = jnp.zeros_like(slot), jnp.zeros_like(slot)
         for k in range(count // NB):
-            owner, row = owner_of[k, 0], row_of[k]
+            owner, row = owner_of[k], row_of[k]
             hot_row = jnp.where(slot == k, place(owner, depth, 0) * 8 + row, hot_row)
             hot_column = jnp.where(slot == k, owner * out_a.shape[0] + row, hot_column)
         to_column = jnp.where(
@@ -272,7 +272,7 @@
     def pick(k, which):
         def index(i, owner_of, row_of, offset_of):
             slot = i * group + k
-            return (row_of[slot], place(owner_of[slot, 0], depth, which), 0, 0)
+            return (row_of[slot], place(owner_of[slot], depth, which), 0, 0)
 
         return pl.BlockSpec((1, 1, HALF, PLANE), index)
 
@@ -398,7 +398,7 @@
             for dz in range(1, depth):
                 total = total + last[row, dz - 1].astype(jnp.float32)
             if stream == 2:
-                ham[...] = total
+                ham[...] = total[:rows]
             else:
                 grad[row, stream * HALF : (stream + 1) * HALF, :] = total
 
@@ -426,7 +426,7 @@
         functools.partial(scatter_kernel, depth, rows),
         out_shape=(
             jax.ShapeDtypeStruct((rows, NB, PLANE), jnp.float32),
-            jax.ShapeDtypeStruct((8, columns), jnp.float32),
+            jax.ShapeDtypeStruct((rows, columns), jnp.float32),
         ),
         in_specs=[pl.BlockSpec(memory_space=pl.ANY)] * 2
         + [pl.BlockSpec(memory_space=pltpu.VMEM)],
@@ -453,10 +453,10 @@
     upper = potential if lax.axis_size("grp") == 1 else passed_along(potential, "grp", -1)
     got_a, got_b = gather(owned_blips.reshape(rows, NB, PLANE), depth)
     part_a, part_b, part_h = domain(
-        got_a, got_b, potential[0], upper[0], slot_owner, slot_row, slot_offset, depth
+        got_a, got_b, potential[0], upper[0], slot_owner.reshape(-1), slot_row, slot_offset, depth
     )
     grad, ham = scatter(part_a, part_b, part_h.reshape(1, devices, 8, -1), depth)
-    return grad.reshape(rows, -1), ham[:rows]
+    return grad.reshape(rows, -1), ham
 
 
 def solution(mesh):

time: 141 us -> 139 us (0.986)
  no operation moved by 1% of the time
where the time goes in v5:
time: 139 us
  Pallas kernels  133 us (96%)
  local copies, waits for them, and re-layouts  5.15 us (4%)
    pallas_call x1, Pallas kernels, scatter(): pl.pallas_call(functools.partial(scatter_kernel, depth, rows), out_shape=...  57.7 us
    pallas_call x1, Pallas kernels, gather(): pl.pallas_call(functools.partial(gather_kernel, depth, rows), out_shape=(...  53.8 us
    pallas_call x1, Pallas kernels, domain(): pl.pallas_call(functools.partial(domain_kernel, group, steps, depth), gri...  21.6 us
    unnamed x3, local copies, waits for them, and re-layouts  5.15 us

profile of v5, /device:TPU:0, one launch (start us, length us, event | category | flops | bytes accessed | tf_op | source)
XLA Modules:
  0.0 138.9 jit_solution(2567411737130527192)
XLA Ops:
  0.6 1.7 %copy.14 = bf16[1,4,32,1024]{3,2,1,0:T(8,128)(2,1)} copy(bf16[1,4,32,1024]{3,1,2,0:T(4,128)(2,1)} %bitcast.14) | data formatting | bytes 524288
  2.4 53.8 %shard_map.104 = (bf16[4,32,16,1024]{3,2,1,0:T(8,128)(2,1)}, bf16[4,32,16,1024]{3,2,1,0:T(8,128)(2,1)}) custom-call(bf16[4,32,1024]{2,1,0:T(8,128)(2,1)} %bitcast.9), custom_call_target="tpu_custom_call" | custom-call | tf_op jit(solution)/shard_map/pallas_call | solution.py:142
  56.2 21.6 %shard_map.105 = (bf16[4,32,16,1024]{3,2,1,0:T(8,128)(2,1)}, bf16[4,32,16,1024]{3,2,1,0:T(8,128)(2,1)}, f32[256,128]{1,0:T(8,128)}) custom-call(s32[24]{0:T(128)} %bitcast.16, s32[24]{0:T(128)} %row_of.1, s32[24]{0:T(128)} %offset_of.1, bf16[4,32,16,1024]{3,2,1,0:T(8,128)(2,1)} %get-tuple-element.9.refs_0_.refs_1_.refs_2_.refs_3_.refs_4_.refs_5_.refs_6_.refs_7_, ...), custom_call_target="tpu_custom_call" | custom-call | flops 6442450944 | bytes 16777216 | tf_op jit(solution)/shard_map/pallas_call | solution.py:293
  77.8 57.7 %shard_map.106 = (f32[4,32,1024]{2,1,0:T(8,128)}, f32[4,128]{1,0:T(4,128)}) custom-call(bf16[4,32,16,1024]{3,2,1,0:T(8,128)(2,1)} %get-tuple-element.11.part_a, bf16[4,32,16,1024]{3,2,1,0:T(8,128)(2,1)} %get-tuple-element.12.part_b, f32[1,32,8,128]{3,2,1,0:T(8,128)} %bitcast.15), custom_call_target="tpu_custom_call" | custom-call | tf_op jit(solution)/shard_map/pallas_call | solution.py:425
  135.5 2.2 %copy.12 = f32[1,4,32,1024]{3,1,2,0:T(4,128)} copy(f32[1,4,32,1024]{3,2,1,0:T(8,128)} %bitcast.13) | data formatting | bytes 1048576
  137.6 1.2 copy.16
